TPU v7x, 512 devices: a whole 4x4x16 slice. The times are simulated.
512 devices in a mesh: row: 16 (over y, x_hi, core), col: 32 (over z, x_lo).
Axes of the slice: x: 4 (x_hi: 2, x_lo: 2; x = x_hi * 2 + x_lo), y: 4, z: 16, core: 2. Of those that a mesh axis runs over, the one named last changes fastest.
Arguments:
- ancestor_inverse: float32 [4096, 4096], P('row', 'col'), may hold values from -6 to 6
- pattern: int32 [32, 32], replicated, may hold values 0 or 1
- listed: int32 [2, 16], replicated, may hold values from 0 to 31, as said below
- panels: float32 [2, 4096, 512], P(None, ('col', 'row')), may hold values from -0.09375 to 0.09375
- parent_panels: float32 [1, 512, 512], replicated, may hold values from -0.25 to 0.25
- diag_inverse: float32 [2, 512, 512], P(None, 'row', 'col'), may hold values from -6 to 6
Outputs:
- upper_blocks: float32 [2, 4096, 512], P(None, ('col', 'row'))
- diagonal_blocks: float32 [2, 512, 512], P(None, 'row', 'col')
Inputs may be any that keep to these rules, and one draw needn't show every extreme that they name: Each row of listed names 16 different blocks.
All inputs are finite; a program needn't handle non-finite values.
Results may differ from a plain program's by a relative error of at most 0.00011.
Values sent between devices are 32-bit elements; how exact they have to be, the bound alone decides.
A program may use at most 64 MiB of HBM per device.

v0:
```python
import jax
import jax.numpy as jnp
from jax import lax
from jax.sharding import PartitionSpec as P

BLK = 128


def broadcast(value, axis, source):
    kept = jnp.where(lax.axis_index(axis) == source, value, 0).astype(value.dtype)
    return lax.psum(kept, axis)


def contract_rows(left, right):
    return lax.dot_general(
        left,
        right,
        (((0,), (0,)), ((), ())),
        precision=lax.Precision.HIGHEST,
        preferred_element_type=jnp.float32,
    )


def local(ancestor_inverse, pattern, listed, panels, parent_panels, diag_inverse):
    highest = lax.Precision.HIGHEST
    rows_here, cols_here = ancestor_inverse.shape
    row_count = lax.axis_size("row")
    col_count = lax.axis_size("col")
    column_ratio = col_count // row_count
    row_index = lax.axis_index("row")
    col_index = lax.axis_index("col")
    super_count, shard_rows, panel_width = panels.shape
    row_tiles = rows_here // BLK
    col_tiles = cols_here // BLK
    blocks = pattern.shape[0]
    tile_mask = lax.dynamic_slice(
        pattern, (row_index * row_tiles, col_index * col_tiles), (row_tiles, col_tiles)
    ).astype(jnp.float32)
    masked = (
        ancestor_inverse.reshape(row_tiles, BLK, col_tiles, BLK) * tile_mask[:, None, :, None]
    ).reshape(rows_here, cols_here)
    block_ids = jnp.arange(blocks, dtype=jnp.int32)
    listed_flags = jnp.any(listed[:, :, None] == block_ids[None, None, :], axis=1).astype(
        jnp.float32
    )
    first_row = (col_index * row_count + row_index) * shard_rows
    shard_blocks = (first_row + jnp.arange(shard_rows, dtype=jnp.int32)) // BLK
    onehot = (shard_blocks[:, None] == block_ids[None, :]).astype(jnp.float32)
    row_keep = jnp.dot(
        listed_flags, onehot.T, precision=highest, preferred_element_type=jnp.float32
    )
    kept_panels = panels * row_keep[:, :, None]
    tile_rows = panel_width // row_count
    tile_cols = panel_width // col_count
    uppers = []
    diagonals = []
    previous_upper = None
    previous_tile = None
    for supernode in range(super_count):
        column_slab = lax.all_gather(kept_panels[supernode], "row", axis=0, tiled=True)
        pieces = [
            broadcast(column_slab, "col", column_ratio * row_index + member)
            for member in range(column_ratio)
        ]
        row_slab = jnp.concatenate(pieces, axis=0)
        column_sum = lax.psum_scatter(
            contract_rows(masked, row_slab), "row", scatter_dimension=0, tiled=True
        )
        if supernode > 0:
            parent_link = parent_panels[supernode - 1]
            chained = jnp.dot(
                previous_upper, parent_link, precision=highest, preferred_element_type=jnp.float32
            )
            column_sum = column_sum + chained
        upper_part = -column_sum * row_keep[supernode][:, None]
        partial_value = -contract_rows(kept_panels[supernode], upper_part)
        if supernode > 0:
            partial_value = partial_value + contract_rows(chained, kept_panels[supernode])
            link_band = lax.dynamic_slice_in_dim(parent_link, row_index * tile_rows, tile_rows, 0)
            link_slice = lax.dynamic_slice_in_dim(parent_link, col_index * tile_cols, tile_cols, 0)
            inner = jnp.dot(
                previous_tile, link_slice, precision=highest, preferred_element_type=jnp.float32
            )
            partial_value = partial_value + contract_rows(link_band, inner)
        partial_value = lax.dynamic_update_slice(
            partial_value,
            lax.dynamic_slice(
                partial_value,
                (row_index * tile_rows, col_index * tile_cols),
                (tile_rows, tile_cols),
            )
            + diag_inverse[supernode],
            (row_index * tile_rows, col_index * tile_cols),
        )
        row_band = lax.psum_scatter(partial_value, "row", scatter_dimension=0, tiled=True)
        diag_tile = lax.psum_scatter(row_band, "col", scatter_dimension=1, tiled=True)
        previous_upper = upper_part
        previous_tile = diag_tile
        uppers.append(upper_part)
        diagonals.append(diag_tile)
    return (jnp.stack(uppers), jnp.stack(diagonals))


def solution(mesh):
    return jax.shard_map(
        local,
        mesh=mesh,
        in_specs=(
            P("row", "col"),
            P(),
            P(),
            P(None, ("col", "row"), None),
            P(),
            P(None, "row", "col"),
        ),
        out_specs=(P(None, ("col", "row"), None), P(None, "row", "col")),
        check_vma=False,
    )
```

profile of v0, /device:TPU:16, one launch (start us, length us, event | category | flops | bytes accessed | tf_op | source)
XLA Modules:
  0.0 977.3 jit_solution(14819293796184799126)
XLA Ops:
  7.3 0.7 copy-done.9
  8.4 21.0 %all-gather = f32[1,128,512]{2,1,0:T(8,128)S(1)} all-gather(f32[1,8,512]{2,1,0:T(8,128)S(1)} %get-tuple-element.10), channel_id=2, replica_groups=mesh['row'=16,'col'=32] {'row'}, dimensions={1}, use_global_device_ids=true | all-gather | bytes 278528 | tf_op jit(solution)/shard_map/all_gather | solution.py:60
  29.4 23.9 %all-gather.1 = f32[1,128,512]{2,1,0:T(8,128)S(1)} all-gather(f32[1,8,512]{2,1,0:T(8,128)S(1)} %get-tuple-element.11), channel_id=3, replica_groups=mesh['row'=16,'col'=32] {'row'}, dimensions={1}, use_global_device_ids=true | all-gather | bytes 278528 | tf_op jit(solution)/shard_map/all_gather | solution.py:60
  53.3 0.9 select_bitcast_fusion.1
  54.2 0.9 select_bitcast_fusion.3
  55.1 0.9 convert_reduce_fusion
  56.1 267.7 %all-reduce.3.cloned.1.call-done = (f32[128,512]{1,0:T(8,128)}, f32[128,512]{1,0:T(8,128)}, f32[128,512]{1,0:T(8,128)}, f32[128,512]{1,0:T(8,128)}) async-done(((f32[128,512]{1,0:T(8,128)}, f32[128,512]{1,0:T(8,128)}, f32[128,512]{1,0:T(8,128)}, f32[128,512]{1,0:T(8,128)}), (f32[128,512]{1,0:T(8,128)}, f32[128,512]{1,0:T(8,128)}, f32[128,512]{1,0:T(8,128)}, ...) | async-done | bytes 1048592 | tf_op jit(solution)/shard_map/psum | solution.py:11
  323.8 2.3 fusion.2
  326.2 0.9 copy-done.2
  327.1 1.2 fusion.6
  328.4 85.9 %reduce-scatter.11.cloned.1.call-done = f32[8,512]{1,0:T(8,128)} async-done(((f32[128,512]{1,0:T(8,128)}), f32[8,512]{1,0:T(8,128)}) %reduce-scatter.11.cloned.1.call-update) | async-done | bytes 16400 | tf_op jit(solution)/shard_map/reduce_scatter | solution.py:66
  414.3 1.8 convolution_negate_fusion.1
  416.2 0.7 dynamic_update_slice.6
  416.9 1.3 copy.8
  418.3 0.6 copy-done.4
  418.9 0.6 fusion
  419.5 87.4 %reduce-scatter.13.cloned.1.call-done = f32[8,512]{1,0:T(8,128)} async-done(((f32[128,512]{1,0:T(8,128)}), f32[8,512]{1,0:T(8,128)}) %reduce-scatter.13.cloned.1.call-update) | async-done | bytes 16400 | tf_op jit(solution)/shard_map/reduce_scatter | solution.py:66
  506.9 1.8 convolution_negate_fusion
  508.7 92.5 %reduce-scatter.19.cloned.1.call-done = f32[32,512]{1,0:T(8,128)} async-done(((f32[512,512]{1,0:T(8,128)}), f32[32,512]{1,0:T(8,128)}) %reduce-scatter.19.cloned.1.call-update) | async-done | bytes 65552
  601.3 1.7 copy.9
  603.0 1.0 convolution_add_fusion.1
  604.1 135.6 %reduce-scatter.15.cloned.1.call-done = f32[32,16]{0,1:T(8,128)} async-done(((f32[32,512]{0,1:T(8,128)}), f32[32,16]{0,1:T(8,128)}) %reduce-scatter.15.cloned.1.call-update) | async-done | bytes 2064 | tf_op jit(solution)/shard_map/reduce_scatter | solution.py:96
  739.6 0.9 fusion.16
  740.6 1.0 convolution_add_fusion
  741.7 0.7 dynamic_update_slice.7
  742.4 1.3 copy.10
  743.8 0.6 copy-done.5
  744.5 86.1 %reduce-scatter.21.cloned.1.call-done = f32[32,512]{1,0:T(8,128)} async-done(((f32[512,512]{1,0:T(8,128)}), f32[32,512]{1,0:T(8,128)}) %reduce-scatter.21.cloned.1.call-update) | async-done | bytes 65552
  830.6 1.7 copy.11
  832.4 0.6 pad_maximum_fusion
  833.0 136.1 %reduce-scatter.17.cloned.1.call-done = f32[32,16]{0,1:T(8,128)} async-done(((f32[32,512]{0,1:T(8,128)}), f32[32,16]{0,1:T(8,128)}) %reduce-scatter.17.cloned.1.call-update) | async-done | bytes 2064 | tf_op jit(solution)/shard_map/reduce_scatter | solution.py:96
  969.2 1.3 pad_maximum_fusion.1
  (41 shorter events, 1.2 us)
Async XLA Ops:
  7.2 411.1 %copy-start = (f32[1,512,512]{2,1,0:T(8,128)S(1)}, f32[1,512,512]{2,1,0:T(8,128)}, u32[]{:S(2)}) copy-start(f32[1,512,512]{2,1,0:T(8,128)} %param.10) | copy-start | bytes 3145732
  7.2 316.6 %all-reduce.3.cloned.1.call-start = ((), (), s32[]{:S(2)}) async-start(), calls=%async_computation.12 | async-start | bytes 2097152 | tf_op jit(solution)/shard_map/psum | solution.py:11
  7.2 0.8 copy-start.9
  7.3 1.0 copy-start.6
  55.1 268.8 %copy-start.1 = (f32[256,128]{1,0:T(8,128)S(1)}, f32[256,128]{1,0:T(8,128)}, u32[]{:S(2)}) copy-start(f32[256,128]{1,0:T(8,128)} %param.6) | copy-start | bytes 393220
  55.1 359.2 %reduce-scatter.11.cloned.1.call-start = ((), (), s32[]{:S(2)}) async-start(), calls=%async_computation.6 | async-start | bytes 278528 | tf_op jit(solution)/shard_map/reduce_scatter | solution.py:66
  323.8 2.4 copy-start.3
  326.1 0.9 copy-start.2
  326.1 180.8 %reduce-scatter.13.cloned.1.call-start = ((), (), s32[]{:S(2)}) async-start(), calls=%async_computation.7 | async-start | bytes 278528 | tf_op jit(solution)/shard_map/reduce_scatter | solution.py:66
  328.3 273.0 %reduce-scatter.19.cloned.1.call-start = ((), (), s32[]{:S(2)}) async-start(), calls=%async_computation.10 | async-start | bytes 1114112
  414.3 1.8 copy-start.8
  418.2 0.7 copy-start.4
  418.2 321.4 %reduce-scatter.15.cloned.1.call-start = ((), (), s32[]{:S(2)}) async-start(), calls=%async_computation.8 | async-start | bytes 270336 | tf_op jit(solution)/shard_map/reduce_scatter | solution.py:96
  603.0 227.7 %reduce-scatter.21.cloned.1.call-start = ((), (), s32[]{:S(2)}) async-start(), calls=%async_computation.11 | async-start | bytes 1114112
  743.7 0.7 copy-start.5
  743.7 225.4 %reduce-scatter.17.cloned.1.call-start = ((), (), s32[]{:S(2)}) async-start(), calls=%async_computation.9 | async-start | bytes 270336 | tf_op jit(solution)/shard_map/reduce_scatter | solution.py:96
  832.4 136.7 %copy-start.7 = (f32[32,16]{0,1:T(8,128)S(1)}, f32[32,16]{0,1:T(8,128)}, u32[]{:S(2)}) copy-start(f32[32,16]{0,1:T(8,128)} %reduce-scatter.15.cloned.1.call-done) | copy-start | bytes 6148
Sparse Core Ops, SparseCore 0:
  55.2 268.5 all-reduce.2
  329.0 85.2 reduce-scatter.10
  419.5 87.3 reduce-scatter.12
  512.1 89.1 reduce-scatter.18
  603.9 135.6 reduce-scatter.14
  744.8 85.7 reduce-scatter.20
  833.4 135.6 reduce-scatter.16
where the time goes:
time: 978 us; the launch traced here: 977 us
  waiting for transfers between devices  892 us (91%)
  blocking collectives  44.9 us (5%)
  between operations  14.3 us (1%)
  matrix products  10.9 us (1%)
  local copies, waits for them, and re-layouts  10.3 us (1%)
    reduce_scatter x2, waiting for transfers between devices, local(): lax.psum_scatter(row_band, 'col', scatter_dimension=1, tiled=True)  272 us
    psum x1, waiting for transfers between devices, broadcast(): return lax.psum(kept, axis)  268 us
    unnamed x9, waiting for transfers between devices  179 us
    reduce_scatter x2, waiting for transfers between devices, local(): lax.psum_scatter(contract_rows(masked, row_slab), 'row', scatter_dimensio...  173 us
    all_gather x2, blocking collectives, local(): lax.all_gather(kept_panels[supernode], 'row', axis=0, tiled=True)  44.9 us
  transfers between devices with their start and end apart: 7, of which 7 were waited for; matrix products, arithmetic and copies ran while one was open for 1% of the time, Pallas kernels for 0%

commit v1 on v0

--- a/solution.py
+++ b/solution.py
@@ -8,7 +8,7 @@
 
 def broadcast(value, axis, source):
     kept = jnp.where(lax.axis_index(axis) == source, value, 0).astype(value.dtype)
-    return lax.psum(kept, axis)
+    return jnp.sum(lax.all_gather(kept, axis), axis=0)
 
 
 def contract_rows(left, right):

time: 978 us -> 1470 us (1.50)
  the two profiles are of different devices: /device:TPU:16 before, /device:TPU:8 now
where the time goes in v1:
time: 1470 us
  waiting for transfers between devices  1370 us (93%)
  blocking collectives  48.9 us (3%)
  other arithmetic  23.6 us (2%)
    all_gather x4, waiting for transfers between devices, broadcast(): return jnp.sum(lax.all_gather(kept, axis), axis=0)  747 us
    reduce_scatter x2, waiting for transfers between devices, local(): lax.psum_scatter(row_band, 'col', scatter_dimension=1, tiled=True)  269 us
    unnamed x12, waiting for transfers between devices  181 us
    reduce_scatter x2, waiting for transfers between devices, local(): lax.psum_scatter(contract_rows(masked, row_slab), 'row', scatter_dimensio...  172 us
    all_gather x2, blocking collectives, local(): lax.all_gather(kept_panels[supernode], 'row', axis=0, tiled=True)  48.9 us
  transfers between devices with their start and end apart: 10, of which 10 were waited for; matrix products, arithmetic and copies ran while one was open for 2% of the time, Pallas kernels for 0%

profile of v1, /device:TPU:8, one launch (start us, length us, event | category | flops | bytes accessed | tf_op | source)
XLA Modules:
  0.0 1474.0 jit_solution(6270038458293527624)
XLA Ops:
  9.1 23.1 %all-gather = f32[1,128,512]{2,1,0:T(8,128)S(1)} all-gather(f32[1,8,512]{2,1,0:T(8,128)S(1)} %get-tuple-element.6), channel_id=2, replica_groups=mesh['row'=16,'col'=32] {'row'}, dimensions={1}, use_global_device_ids=true | all-gather | bytes 278528 | tf_op jit(solution)/shard_map/all_gather | solution.py:60
  32.2 0.9 broadcast_select_fusion.3
  33.9 25.8 %all-gather.3 = f32[1,128,512]{2,1,0:T(8,128)S(1)} all-gather(f32[1,8,512]{2,1,0:T(8,128)S(1)} %get-tuple-element.7), channel_id=5, replica_groups=mesh['row'=16,'col'=32] {'row'}, dimensions={1}, use_global_device_ids=true | all-gather | bytes 278528 | tf_op jit(solution)/shard_map/all_gather | solution.py:60
  59.7 0.9 broadcast_select_fusion.1
  61.2 0.9 convert_reduce_fusion
  62.2 169.3 %all-gather.17.cloned.1.call-done = f32[1,4096,512]{2,1,0:T(8,128)} async-done(((f32[1,128,512]{2,1,0:T(8,128)}), f32[1,4096,512]{2,1,0:T(8,128)}) %all-gather.17.cloned.1.call-update) | async-done | bytes 8388624 | tf_op jit(solution)/shard_map/all_gather | solution.py:11
  231.4 4.3 reduce_sum.37
  235.7 193.6 %all-gather.15.cloned.1.call-done = f32[1,4096,512]{2,1,0:T(8,128)} async-done(((f32[1,128,512]{2,1,0:T(8,128)}), f32[1,4096,512]{2,1,0:T(8,128)}) %all-gather.15.cloned.1.call-update) | async-done | bytes 8388624 | tf_op jit(solution)/shard_map/all_gather | solution.py:11
  429.4 4.3 reduce_sum.36
  433.6 1.2 fusion.2
  434.9 191.4 %all-gather.21.cloned.1.call-done = f32[1,4096,512]{2,1,0:T(8,128)} async-done(((f32[1,128,512]{2,1,0:T(8,128)}), f32[1,4096,512]{2,1,0:T(8,128)}) %all-gather.21.cloned.1.call-update) | async-done | bytes 8388624 | tf_op jit(solution)/shard_map/all_gather | solution.py:11
  626.3 4.3 reduce_sum.39
  630.6 192.5 %all-gather.19.cloned.1.call-done = f32[1,4096,512]{2,1,0:T(8,128)} async-done(((f32[1,128,512]{2,1,0:T(8,128)}), f32[1,4096,512]{2,1,0:T(8,128)}) %all-gather.19.cloned.1.call-update) | async-done | bytes 8388624 | tf_op jit(solution)/shard_map/all_gather | solution.py:11
  823.1 4.3 reduce_sum.38
  827.4 1.2 fusion.6
  828.6 85.4 %reduce-scatter.11.cloned.1.call-done = f32[8,512]{1,0:T(8,128)} async-done(((f32[128,512]{1,0:T(8,128)}), f32[8,512]{1,0:T(8,128)}) %reduce-scatter.11.cloned.1.call-update) | async-done | bytes 16400 | tf_op jit(solution)/shard_map/reduce_scatter | solution.py:66
  914.1 1.9 convolution_negate_fusion.1
  916.7 1.3 copy.8
  918.1 1.3 fusion
  919.4 86.4 %reduce-scatter.13.cloned.1.call-done = f32[8,512]{1,0:T(8,128)} async-done(((f32[128,512]{1,0:T(8,128)}), f32[8,512]{1,0:T(8,128)}) %reduce-scatter.13.cloned.1.call-update) | async-done | bytes 16400 | tf_op jit(solution)/shard_map/reduce_scatter | solution.py:66
  1005.8 1.9 convolution_negate_fusion
  1007.7 91.9 %reduce-scatter.19.cloned.1.call-done = f32[32,512]{1,0:T(8,128)} async-done(((f32[512,512]{1,0:T(8,128)}), f32[32,512]{1,0:T(8,128)}) %reduce-scatter.19.cloned.1.call-update) | async-done | bytes 65552
  1099.7 1.7 copy.9
  1101.4 1.0 convolution_add_fusion.1
  1102.4 134.4 %reduce-scatter.15.cloned.1.call-done = f32[32,16]{0,1:T(8,128)} async-done(((f32[32,512]{0,1:T(8,128)}), f32[32,16]{0,1:T(8,128)}) %reduce-scatter.15.cloned.1.call-update) | async-done | bytes 2064 | tf_op jit(solution)/shard_map/reduce_scatter | solution.py:96
  1236.8 0.9 fusion.16
  1237.8 1.0 convolution_add_fusion
  1239.6 1.3 copy.10
  1241.0 87.8 %reduce-scatter.21.cloned.1.call-done = f32[32,512]{1,0:T(8,128)} async-done(((f32[512,512]{1,0:T(8,128)}), f32[32,512]{1,0:T(8,128)}) %reduce-scatter.21.cloned.1.call-update) | async-done | bytes 65552
  1328.8 1.7 copy.11
  1331.2 134.6 %reduce-scatter.17.cloned.1.call-done = f32[32,16]{0,1:T(8,128)} async-done(((f32[32,512]{0,1:T(8,128)}), f32[32,16]{0,1:T(8,128)}) %reduce-scatter.17.cloned.1.call-update) | async-done | bytes 2064 | tf_op jit(solution)/shard_map/reduce_scatter | solution.py:96
  1465.8 1.3 pad_maximum_fusion.1
  (44 shorter events, 6.0 us)
Async XLA Ops:
  7.2 910.9 %copy-start = (f32[1,512,512]{2,1,0:T(8,128)S(1)}, f32[1,512,512]{2,1,0:T(8,128)}, u32[]{:S(2)}) copy-start(f32[1,512,512]{2,1,0:T(8,128)} %param.10) | copy-start | bytes 3145732
  7.2 224.3 %all-gather.17.cloned.1.call-start = ((), (), s32[]{:S(2)}) async-start(), calls=%async_computation.11 | async-start | bytes 8650752 | tf_op jit(solution)/shard_map/all_gather | solution.py:11
  33.1 396.2 %all-gather.15.cloned.1.call-start = ((), (), s32[]{:S(2)}) async-start(), calls=%async_computation.10 | async-start | bytes 8650752 | tf_op jit(solution)/shard_map/all_gather | solution.py:11
  33.9 592.4 %all-gather.21.cloned.1.call-start = ((), (), s32[]{:S(2)}) async-start(), calls=%async_computation.13 | async-start | bytes 8650752 | tf_op jit(solution)/shard_map/all_gather | solution.py:11
  60.6 762.5 %all-gather.19.cloned.1.call-start = ((), (), s32[]{:S(2)}) async-start(), calls=%async_computation.12 | async-start | bytes 8650752 | tf_op jit(solution)/shard_map/all_gather | solution.py:11
  61.2 852.9 %reduce-scatter.11.cloned.1.call-start = ((), (), s32[]{:S(2)}) async-start(), calls=%async_computation.6 | async-start | bytes 278528 | tf_op jit(solution)/shard_map/reduce_scatter | solution.py:66
  231.4 202.2 %copy-start.1 = (f32[256,128]{1,0:T(8,128)S(1)}, f32[256,128]{1,0:T(8,128)}, u32[]{:S(2)}) copy-start(f32[256,128]{1,0:T(8,128)} %param.6) | copy-start | bytes 393220
  434.9 571.0 %reduce-scatter.13.cloned.1.call-start = ((), (), s32[]{:S(2)}) async-start(), calls=%async_computation.7 | async-start | bytes 278528 | tf_op jit(solution)/shard_map/reduce_scatter | solution.py:66
  626.3 289.6 %copy-start.4 = (f32[2,32,16]{1,2,0:T(8,128)S(1)}, f32[2,32,16]{1,2,0:T(8,128)}, u32[]{:S(2)}) copy-start(f32[2,32,16]{1,2,0:T(8,128)} %param.11) | copy-start | bytes 12292
  828.6 271.1 %reduce-scatter.19.cloned.1.call-start = ((), (), s32[]{:S(2)}) async-start(), calls=%async_computation.14 | async-start | bytes 1114112
  914.1 416.4 %copy-start.2 = (f32[8,512]{1,0:T(8,128)S(1)}, f32[8,512]{1,0:T(8,128)}, u32[]{:S(2)}) copy-start(f32[8,512]{1,0:T(8,128)} %reduce-scatter.11.cloned.1.call-done) | copy-start | bytes 49156
  918.0 318.8 %reduce-scatter.15.cloned.1.call-start = ((), (), s32[]{:S(2)}) async-start(), calls=%async_computation.8 | async-start | bytes 270336 | tf_op jit(solution)/shard_map/reduce_scatter | solution.py:96
  1005.8 235.1 %copy-start.3 = (f32[8,512]{1,0:T(8,128)S(1)}, f32[8,512]{1,0:T(8,128)}, u32[]{:S(2)}) copy-start(f32[8,512]{1,0:T(8,128)} %reduce-scatter.13.cloned.1.call-done) | copy-start | bytes 49156
  1101.3 227.5 %reduce-scatter.21.cloned.1.call-start = ((), (), s32[]{:S(2)}) async-start(), calls=%async_computation.15 | async-start | bytes 1114112
  1240.9 224.9 %reduce-scatter.17.cloned.1.call-start = ((), (), s32[]{:S(2)}) async-start(), calls=%async_computation.9 | async-start | bytes 270336 | tf_op jit(solution)/shard_map/reduce_scatter | solution.py:96
Sparse Core Ops, SparseCore 0:
  33.2 198.1 all-gather.16
  233.5 195.7 all-gather.14
  431.4 194.8 all-gather.20
  628.2 194.8 all-gather.18
  827.5 86.5 reduce-scatter.10
  918.5 87.3 reduce-scatter.12
  1010.5 89.1 reduce-scatter.18
  1102.7 134.1 reduce-scatter.14
  1241.5 87.2 reduce-scatter.20
  1331.7 134.1 reduce-scatter.16
